TPU v7x, 256 devices: a whole 4x4x8 slice. The times are simulated.
256 devices in a mesh: bx: 4 (over x), by: 4 (over y), vert: 16 (over z, core).
Axes of the slice: x: 4, y: 4, z: 8, core: 2. Of those that a mesh axis runs over, the one named last changes fastest.
Arguments:
- estimate: float32 [128, 128, 512], P('bx', 'by', 'vert'), may hold values from 0.5 to 1.5
- view_tiles: bfloat16 [4, 4, 16, 64, 64, 128], P('bx', 'by', 'vert'), may hold values from 0.19921875 to 2
- slot_view: int32 [4, 4, 4], P('bx', 'by'), may hold values from 0 to 3, each once within a row
- psf_taps: float32 [4, 3, 3, 33], replicated, may hold values from 0.05 to 1
Outputs:
- refined: float32 [128, 128, 512], P('bx', 'by', 'vert')
Inputs may be any that keep to these rules, and one draw needn't show every extreme that they name: `slot_view`: each block's list names every view once.
All inputs are finite; a program needn't handle non-finite values.
Results may differ from a plain program's by a relative error of at most 0.0003.
Values may be sent and summed in bfloat16 or wider, within the bound.
A program may use at most 128 MiB of HBM per device.

v0:
```python
import jax
import jax.numpy as jnp
from jax import lax
from jax.experimental import pallas as pl
from jax.experimental.pallas import tpu as pltpu
from jax.sharding import PartitionSpec as P

BACKGROUND = 0.1
MESH = pl.DeviceIdType.MESH
F32, BF16 = jnp.float32, jnp.bfloat16
BLOCK = 32
RAD = 16
TAPS = 33
RANK = 3
VIEWS = 4
GROUPS = 4
LANES = 128


def iota(shape, axis):
    return lax.broadcasted_iota(jnp.int32, shape, axis)


def dot(a, b):
    return jnp.dot(a, b, preferred_element_type=F32)


def build_taps(psf, slot_view, slot, taps):
    listed = slot_view[...]
    view = jnp.sum(jnp.where(iota(listed.shape, 2) == slot, listed, 0), axis=2, keepdims=True)
    held = iota((VIEWS, TAPS), 0) == view[0]
    mine = jnp.sum(jnp.where(held[None, None], psf[...], 0.0), axis=2)
    mine = (mine / jnp.sum(mine, axis=-1, keepdims=True)).astype(BF16).astype(F32)
    taps[...] = jnp.zeros_like(taps)
    for a in range(3):
        taps[0, 8 * a : 8 * a + RANK, :TAPS] = mine[a]
    flip = (iota((LANES, LANES), 0) + iota((LANES, LANES), 1) == TAPS - 1).astype(BF16)
    taps[1] = dot(taps[0].astype(BF16), flip)


def band(line, rows, start):
    line = jnp.broadcast_to(line, (rows, LANES))
    return pltpu.roll(line, start % LANES, 1, stride=1, stride_axis=0)


def build_z(taps, q, wz, wb):
    z_in, z_out = iota((LANES, LANES), 0), iota((LANES, LANES), 1)
    near = jnp.abs(z_in - z_out) <= RAD
    rim, out = iota((32, LANES), 0), iota((32, LANES), 1)
    rim_ok = ((rim < RAD) & (out <= rim) & (q > 0)) | ((rim >= RAD) & (out >= rim + 96) & (q < 3))
    lane16 = iota((16, LANES), 1)
    for r in range(RANK):
        forward, backward = taps[1, 16 + r : 17 + r, :], taps[0, 16 + r : 17 + r, :]
        columns = slice(r * LANES, (r + 1) * LANES)
        wz[0:128, columns] = jnp.where(near, band(forward, LANES, -RAD), 0.0).astype(BF16)
        wz[128:160, columns] = jnp.where(rim_ok, band(forward, 32, 96), 0.0).astype(BF16)
        wz[160:256, columns] = jnp.zeros((96, LANES), BF16)
        main = jnp.where(near, band(backward, LANES, -RAD), 0.0)
        low = jnp.where((lane16 < RAD) & (q > 0), band(backward, 16, 0), 0.0)
        high = jnp.where((lane16 < RAD) & (q < 3), band(backward, 16, 96), 0.0)
        high = pltpu.roll(high, RAD, 1)
        for g in range(GROUPS):
            wb[g, r * 128 : r * 128 + 128, 0:128] = (
                pltpu.roll(main, 32 * g, 1) if g else main
            ).astype(BF16)
            wb[g, r * 128 : r * 128 + 128, 128:256] = jnp.zeros((128, LANES), BF16)
            lo, hi = (pltpu.roll(m, 32 * g, 1) if g else m for m in (low, high))
            wb[g, r * 128 : r * 128 + 16, 128:256] = lo.astype(BF16)
            wb[g, r * 128 + 112 : r * 128 + 128, 128:256] = hi.astype(BF16)


def build_x(taps, bx, tx, txb):
    spread = (iota((LANES, 384), 1) == 8 * iota((LANES, 384), 0)).astype(BF16)
    past = iota((LANES, LANES), 1) >= iota((LANES, LANES), 0)
    none = jnp.zeros((LANES, LANES), BF16)
    low, high = bx > 0, bx < 3

    def tiles(line):
        turned = [band(line[:, i * LANES : (i + 1) * LANES], LANES, 0) for i in range(3)]
        before = [0.0, turned[0], turned[1]]
        return [jnp.where(past, turned[i], before[i]) for i in range(3)]

    def put(ref, kept):
        for half in range(2):
            for at in range(4):
                here = none
                if 0 <= at - half < 3:
                    here = jnp.where(kept[at], kept_tiles[at - half], 0.0).astype(BF16)
                ref[half * 128 : half * 128 + 128, at * 128 : at * 128 + 128] = here

    wide = [dot(taps[k, 0:8, :].astype(BF16), spread) for k in range(2)]
    for r in range(RANK):
        kept_tiles = tiles(wide[0][r : r + 1])
        put(tx.at[r], (True, True, True, True))
        kept_tiles = tiles(wide[1][r : r + 1])
        put(txb.at[r], (low, True, True, high))


def build_y(taps, by, ty, tyb):
    def inside(rows, first):
        place = by * BLOCK - first + iota((rows, LANES), 1)
        return (place >= 0) & (place < 4 * BLOCK)

    plain = [
        jnp.where(inside(64, 2 * RAD), band(taps[0, 8 + r : 9 + r, :], 64, 0), 0.0) for r in range(RANK)
    ] + [
        jnp.where(inside(32, RAD), band(taps[1, 8 + r : 9 + r, :], 32, 0), 0.0) for r in range(RANK)
    ]
    plain = jnp.concatenate(plain, axis=0).astype(BF16)
    y, column = iota((LANES, 256), 0), iota((LANES, 256), 1)
    parts = [
        dot(plain, (column == 16 * (y // 8) + 8 * k + y % 8).astype(BF16)).reshape(36, 8, 256)
        for k in range(2)
    ]
    both = jnp.stack(parts, axis=1).reshape(36 * 16, 256).astype(BF16)
    for r in range(RANK):
        ty[r] = both[r * 128 : (r + 1) * 128]
    tyb[...] = both[384:576, 0:128]


def kernel(
    est_hbm, tile_hbm, psf_hbm, slot_view_hbm, refined,
    est, tile, psf, slot_view,
    packed, parts, field, after_z, after_x, back_y, back_x, sums, rims,
    got_core, got_rim, got_chip, got_edge,
    taps, tx, ty, wz, tyb, txb, wb,
    load_sem, part_send, part_recv, face_send, face_recv, core_send, core_recv, sum_send, sum_recv,
):
    bx, by, vert = lax.axis_index("bx"), lax.axis_index("by"), lax.axis_index("vert")
    q, slot = vert // VIEWS, vert % VIEWS
    core, chip = slot % 2, slot // 2

    loads = [
        pltpu.make_async_copy(source, target, load_sem.at[i])
        for i, (source, target) in enumerate(
            ((est_hbm, est), (psf_hbm, psf), (slot_view_hbm, slot_view), (tile_hbm, tile))
        )
    ]
    for copy in loads:
        copy.start()

    def at_vert(index):
        return {"vert": index}

    partner = at_vert(q * 4 + chip * 2 + 1 - core)
    x_up, x_down = ({"bx": bx + 1}, bx < 3), ({"bx": bx - 1}, bx > 0)
    y_up, y_down = ({"by": by + 1}, by < 3), ({"by": by - 1}, by > 0)
    above, below = q < 3, q > 0
    first, last = slot == 0, slot == VIEWS - 1
    is_edge = (first & below) | (last & above)

    def exists(jy, jx):
        here = jy == jy
        for index, j in ((by, jy), (bx, jx)):
            if j != 1:
                here = (index > 0 if j == 0 else index < 3) & here
        return here

    got_edge[...] = jnp.zeros_like(got_edge)
    barrier = pltpu.get_barrier_semaphore()

    def greet(device):
        pl.semaphore_signal(barrier, inc=1, device_id=device, device_id_type=MESH)

    for k in range(1, VIEWS):
        greet(at_vert(q * 4 + (slot + k) % VIEWS))
    for device, there in (x_up, x_down, y_up, y_down):
        pl.when(there)(lambda device=device: greet(device))

    @pl.when(below)
    def _():
        greet(at_vert(vert - slot - 1))
        pl.when(first)(lambda: greet(at_vert(vert - 3)))

    @pl.when(above)
    def _():
        greet(at_vert(vert - slot + 4))
        pl.when(last)(lambda: greet(at_vert(vert + 3)))

    loads[0].wait()
    groups = est[...].reshape(BLOCK, GROUPS, 8, BLOCK)
    line = jnp.concatenate([groups[:, g].reshape(256, BLOCK) for g in range(GROUPS)], axis=1)
    packed[...] = pltpu.roll(line, slot * 32, 1).astype(BF16)

    beside = [(there, 1) for _, there in (x_up, x_down, y_up, y_down)] + [(is_edge, 4)]
    beside += [((slot == 1) & above, 1), ((slot == 2) & below, 1)]
    pl.semaphore_wait(barrier, 3 + sum(jnp.where(there, n, 0) for there, n in beside))

    def part_copy(dst_index, send, device, half):
        return pltpu.make_async_remote_copy(
            src_ref=packed.at[pl.ds(half * 128, 128), :], dst_ref=parts.at[dst_index],
            send_sem=part_send.at[send], recv_sem=part_recv.at[dst_index],
            device_id=device, device_id_type=MESH,
        )

    for k in range(1, VIEWS):
        other = (slot + k) % VIEWS
        part_copy(slot, k - 1, at_vert(q * 4 + other), other % 2).start()

    @pl.when(last & above)
    def _():
        for k in range(VIEWS):
            part_copy(4, 3 + k, at_vert(vert + 1 + k), k % 2).start()

    @pl.when(first & below)
    def _():
        for k in range(VIEWS):
            part_copy(5, 3 + k, at_vert(vert - 4 + k), k % 2).start()

    parts[slot] = packed[pl.ds(core * 128, 128), :]

    def clear(ref):
        ref[...] = jnp.zeros(ref.shape, BF16)

    pl.when(~below)(lambda: clear(parts.at[4]))
    pl.when(~above)(lambda: clear(parts.at[5]))
    pl.when(bx == 0)(lambda: clear(field.at[:, :, 0:256, :]))
    pl.when(bx == 3)(lambda: clear(field.at[:, :, 512:768, :]))
    pl.when(by == 0)(lambda: clear(field.at[0]))
    pl.when(by == 3)(lambda: clear(field.at[2]))
    loads[1].wait()
    loads[2].wait()
    build_taps(psf, slot_view, slot, taps)
    build_z(taps, q, wz, wb)

    for k in range(1, VIEWS):
        part_copy((slot + k) % VIEWS, 0, partner, 0).wait_recv()
    for k, there in ((4, below), (5, above)):
        pl.when(there)(lambda k=k: part_copy(k, 0, partner, 0).wait_recv())

    chunk = iota((128, LANES), 1) // 32
    own_rows = pl.ds(256 + core * 128, 128)
    have = [parts[k].astype(F32) for k in range(6)]
    for g in range(GROUPS):
        line = have[(3 - g) % 4]
        for at in range(3):
            line = jnp.where(chunk == at, have[(at - g) % 4], line)
        if g:
            line = pltpu.roll(line, LANES - 32 * g, 1)
        field[1, g, own_rows, :] = line.astype(BF16)
    is_high = iota((128, LANES), 1) % 32 < RAD
    line = pltpu.roll(jnp.where(is_high, have[5], have[4]), RAD, 1)
    field[1, 4, own_rows, :] = line.astype(BF16)

    def piece(jy, jx, tp, owner):
        return field.at[jy, :, pl.ds(jx * 256 + owner * 128 + tp * 64, 64), :]

    def number(jy, jx, tp):
        return (jy * 3 + jx) * 2 + tp

    def face_copy(source, target, tp, send, device):
        return pltpu.make_async_remote_copy(
            src_ref=piece(*source, tp, core), dst_ref=piece(*target, tp, core),
            send_sem=face_send.at[send], recv_sem=face_recv.at[number(*target, tp)],
            device_id=device, device_id_type=MESH,
        )

    def core_copy(jy, jx, tp, owner):
        return pltpu.make_async_remote_copy(
            src_ref=piece(jy, jx, tp, owner), dst_ref=piece(jy, jx, tp, owner),
            send_sem=core_send.at[number(jy, jx, tp)], recv_sem=core_recv.at[number(jy, jx, tp)],
            device_id=partner, device_id_type=MESH,
        )

    faces = []

    def send_face(source, target, tp, way):
        device, there = way
        copy = face_copy(source, target, tp, len(faces), device)
        there = there & exists(*source)
        pl.when(there)(copy.start)
        faces.append((copy, there))

    def arrived(jy, jx, tp):
        @pl.when(exists(jy, jx))
        def _():
            face_copy((jy, jx), (jy, jx), tp, 0, partner).wait_recv()
            core_copy(jy, jx, tp, core).start()

    def swapped(jy, jx):
        @pl.when(exists(jy, jx))
        def _():
            for tp in range(2):
                core_copy(jy, jx, tp, 1 - core).wait_recv()

    def forward_z(jy, jx):
        rows = pl.ds(jx * 256, 256)
        rim = field[jy, 4, rows, :]
        for g in range(GROUPS):
            turned = pltpu.roll(rim, LANES - 32 * g, 1) if g else rim
            done = dot(jnp.concatenate([field[jy, g, rows, :], turned], axis=1), wz[...])
            for r in range(RANK):
                after_z[r, jy * GROUPS + g, rows, :] = done[:, r * 128 : (r + 1) * 128].astype(BF16)

    def forward_x(jy):
        def body(step, carry):
            r, group = step // 2, jy * GROUPS + step % 2 * 2
            for b in range(2):
                rows = pl.ds(b * 256, 512)
                both = jnp.concatenate([after_z[r, group + k, rows, :] for k in range(2)], axis=1)
                done = dot(tx[r], both).astype(BF16)
                for k in range(2):
                    after_x[r, group + k, b * 256 : b * 256 + 256, :] = done[:, k * 128 : k * 128 + 128]
            return carry

        lax.fori_loop(0, 2 * RANK, body, 0, unroll=True)

    for first_tp in (0, 1):
        send_face((1, 1), (1, 0), first_tp, x_up)
        send_face((1, 1), (1, 2), first_tp, x_down)
        send_face((1, 1), (0, 1), 1 - first_tp, y_up)
        send_face((1, 1), (2, 1), 1 - first_tp, y_down)
    for tp in (0, 1):
        core_copy(1, 1, tp, core).start()
    build_x(taps, bx, tx, txb)
    for side in (0, 2):
        arrived(1, side, 0)
        send_face((1, side), (0, side), 0, y_up)
        send_face((1, side), (2, side), 0, y_down)
        arrived(side, 1, 1)
        send_face((side, 1), (side, 0), 1, x_up)
        send_face((side, 1), (side, 2), 1, x_down)
    build_y(taps, by, ty, tyb)
    swapped(1, 1)
    forward_z(1, 1)
    for side in (0, 2):
        arrived(1, side, 1)
        arrived(side, 1, 0)
    for side in (0, 2):
        swapped(1, side)
        forward_z(1, side)
        swapped(side, 1)
        forward_z(side, 1)
    forward_x(1)
    for jy in (0, 2):
        for jx in (0, 2):
            for tp in range(2):
                arrived(jy, jx, tp)
    for jy in (0, 2):
        for jx in (0, 2):
            swapped(jy, jx)
            forward_z(jy, jx)
        forward_x(jy)

    loads[3].wait()

    def along_y(step, carry):
        blurred = None
        for r in range(RANK):
            both = [
                after_x[r, :, pl.ds(32 * step + 16 * k, 16), :].reshape(192, LANES) for k in range(2)
            ]
            part = dot(ty[r, :, 0:192], jnp.concatenate(both, axis=1))
            blurred = part if blurred is None else blurred + part
        seen = []
        for k in range(2):
            pair = [tile[4 * step + 2 * k + i].astype(F32).reshape(8, 8, LANES) for i in range(2)]
            seen.append(jnp.stack(pair, axis=1).reshape(128, LANES))
        seen = jnp.concatenate(seen, axis=1)
        quotient = (RANK * seen / (blurred + RANK * BACKGROUND)).astype(BF16)
        done = dot(tyb[...], quotient).astype(BF16)
        for k in range(2):
            back_y[:, pl.ds(32 * step + 16 * k, 16), :] = done[:, k * 128 : k * 128 + 128].reshape(
                12, 16, LANES
            )
        return carry

    def backward(half):
        rows, within = slice(half * 128, half * 128 + 128), slice(half * 128, half * 128 + 384)
        rim_sum = None
        for pair in range(2):
            for r in range(RANK):
                at = r * GROUPS + 2 * pair
                both = jnp.concatenate([back_y[at, within, :], back_y[at + 1, within, :]], axis=1)
                done = dot(txb[r, rows, within], both).astype(BF16)
                for k in range(2):
                    back_x[2 * pair + k, rows, r * 128 : (r + 1) * 128] = done[:, k * 128 : k * 128 + 128]
            for g in (2 * pair, 2 * pair + 1):
                done = dot(back_x[g, rows, :], wb[g])
                for c in range(4):
                    at = (g + c) % 4
                    sums[half, c, :, at * 32 : at * 32 + 32] = done[:, at * 32 : at * 32 + 32]
                rim_sum = done[:, LANES:] if rim_sum is None else rim_sum + done[:, LANES:]
        return rim_sum

    far = (1 - chip) * 2 + core

    def sum_copy(source, target, index, device):
        return pltpu.make_async_remote_copy(
            src_ref=source, dst_ref=target, send_sem=sum_send.at[index],
            recv_sem=sum_recv.at[index], device_id=device, device_id_type=MESH,
        )

    far_swap = [
        sum_copy(sums.at[h, (1 - chip) * 2 + 1 - core], got_core.at[h, 0], h, partner) for h in range(2)
    ]
    near_swap = [
        sum_copy(sums.at[h, chip * 2 + 1 - core], got_core.at[h, 1], 2 + h, partner) for h in range(2)
    ]
    over = [sum_copy(sums.at[h, far], got_chip.at[h], 4 + h, at_vert(q * 4 + far)) for h in range(2)]
    rim_swap = sum_copy(rims.at[1 - core], got_rim, 6, partner)
    edge_home = jnp.where(core == 0, vert - slot - 1, vert - slot + 4)
    edge_there = jnp.where(core == 0, q, 3 - q) > 0

    def edge_copy(which):
        return pltpu.make_async_remote_copy(
            src_ref=rims.at[core], dst_ref=got_edge.at[which], send_sem=sum_send.at[7],
            recv_sem=sum_recv.at[7 + which], device_id=at_vert(edge_home), device_id_type=MESH,
        )

    def pass_over(h):
        far_swap[h].wait_recv()
        sums[h, far] = sums[h, far] + got_core[h, 0]
        over[h].start()

    lax.fori_loop(0, 12, along_y, 0, unroll=4)
    top = backward(0)
    far_swap[0].start()
    near_swap[0].start()
    lax.fori_loop(12, 16, along_y, 0, unroll=4)
    pass_over(0)
    bottom = backward(1)
    far_swap[1].start()
    is_low = iota((128, LANES), 1) % 32 < RAD
    rims[0] = jnp.where(is_low, top, pltpu.roll(bottom, RAD, 1))
    rims[1] = jnp.where(is_low, pltpu.roll(top, LANES - RAD, 1), bottom)
    rim_swap.start()
    near_swap[1].start()
    pass_over(1)
    rim_swap.wait_recv()
    rims[core] = rims[core] + got_rim[...]
    pl.when(edge_there)(lambda: edge_copy(chip).start())

    mine = []
    for h in range(2):
        near_swap[h].wait_recv()
        mine.append(sums[h, slot] + got_core[h, 1])
    for h in range(2):
        over[h].wait_recv()
        mine[h] = mine[h] + got_chip[h]

    @pl.when(is_edge)
    def _():
        edge_copy(0).wait_recv()
        edge_copy(1).wait_recv()

    edge = got_edge[0] + got_edge[1]
    start = jnp.where(last, RAD, 0)
    lane = iota((128, LANES), 1)
    keep = is_edge & (lane >= start) & (lane < start + RAD)
    for g in range(GROUPS):
        for h in range(2):
            rim = pltpu.roll(edge, (start + 2 * LANES - RAD * h - 32 * g) % LANES, 1)
            own = pltpu.roll(mine[h], (8 - g - slot) % 4 * 32, 1) + jnp.where(keep, rim, 0.0)
            at = (slice(16 * h, 16 * h + 16), slice(g * 8, g * 8 + 8))
            refined[at] = est[at] * (own[:, 0:BLOCK].reshape(16, 8, BLOCK) * (1.0 / (RANK * VIEWS)))

    for k in range(1, VIEWS):
        part_copy(slot, k - 1, partner, 0).wait_send()

    @pl.when(is_edge)
    def _():
        for k in range(VIEWS):
            part_copy(4, 3 + k, partner, 0).wait_send()

    for copy, there in faces:
        pl.when(there)(copy.wait_send)
    for jy in range(3):
        for jx in range(3):

            @pl.when(exists(jy, jx))
            def _():
                for tp in range(2):
                    core_copy(jy, jx, tp, core).wait_send()

    for copy in far_swap + near_swap + over + [rim_swap]:
        copy.wait_send()
    pl.when(edge_there)(lambda: edge_copy(0).wait_send())


def local(estimate, view_tiles, slot_view, psf_taps):
    vmem = pl.BlockSpec(memory_space=pltpu.VMEM)
    hbm = pl.BlockSpec(memory_space=pltpu.HBM)
    tile = view_tiles[0, 0, 0]
    psf = jnp.transpose(psf_taps, (1, 2, 0, 3))
    scratch = [
        pltpu.VMEM(estimate.shape, F32),
        pltpu.VMEM(tile.shape, BF16),
        pltpu.VMEM(psf.shape, F32),
        pltpu.VMEM(slot_view.shape, jnp.int32),
        pltpu.VMEM((256, LANES), BF16),
        pltpu.VMEM((6, 128, LANES), BF16),
        pltpu.VMEM((3, 5, 768, LANES), BF16),
        pltpu.VMEM((RANK, 12, 768, LANES), BF16),
        pltpu.VMEM((RANK, 12, 512, LANES), BF16),
        pltpu.VMEM((12, 512, LANES), BF16),
        pltpu.VMEM((GROUPS, 256, RANK * LANES), BF16),
        pltpu.VMEM((2, 4, 128, LANES), F32),
        pltpu.VMEM((2, 128, LANES), F32),
        pltpu.VMEM((2, 2, 128, LANES), F32),
        pltpu.VMEM((128, LANES), F32),
        pltpu.VMEM((2, 128, LANES), F32),
        pltpu.VMEM((2, 128, LANES), F32),
        pltpu.VMEM((2, 24, LANES), F32),
        pltpu.VMEM((RANK, 256, 512), BF16),
        pltpu.VMEM((RANK, 128, 256), BF16),
        pltpu.VMEM((256, RANK * LANES), BF16),
        pltpu.VMEM((192, LANES), BF16),
        pltpu.VMEM((RANK, 256, 512), BF16),
        pltpu.VMEM((GROUPS, RANK * LANES, 256), BF16),
        pltpu.SemaphoreType.DMA((4,)),
        pltpu.SemaphoreType.DMA((7,)),
        pltpu.SemaphoreType.DMA((6,)),
        pltpu.SemaphoreType.DMA((16,)),
        pltpu.SemaphoreType.DMA((18,)),
        pltpu.SemaphoreType.DMA((18,)),
        pltpu.SemaphoreType.DMA((18,)),
        pltpu.SemaphoreType.DMA((8,)),
        pltpu.SemaphoreType.DMA((9,)),
    ]
    return pl.pallas_call(
        kernel,
        out_shape=jax.ShapeDtypeStruct(estimate.shape, F32),
        in_specs=[hbm] * 4,
        out_specs=vmem,
        scratch_shapes=scratch,
        compiler_params=pltpu.CompilerParams(
            collective_id=0, has_side_effects=True, vmem_limit_bytes=64 * 1024 * 1024
        ),
    )(estimate, tile, psf, slot_view)


def solution(mesh):
    placed = (
        P("bx", "by", "vert"),
        P("bx", "by", "vert", None, None, None),
        P("bx", "by", None),
        P(),
    )
    return jax.shard_map(
        local, mesh=mesh, in_specs=placed, out_specs=P("bx", "by", "vert"), check_vma=False
    )
```

profile of v0, /device:TPU:47, one launch (start us, length us, event | category | flops | bytes accessed | tf_op | source)
XLA Modules:
  0.0 38.9 jit_solution(1012424408977888286)
XLA Ops:
  0.0 37.0 %shard_map.46 = f32[32,32,32]{2,1,0:T(8,128)} custom-call(f32[32,32,32]{2,1,0:T(8,128)} %est_hbm.1, bf16[64,64,128]{2,1,0:T(8,128)(2,1)} %bitcast.2, f32[3,3,4,33]{3,2,1,0:T(4,128)} %bitcast.3, s32[1,1,4]{2,1,0:T(1,128)} %slot_view_hbm.1), custom_call_target="tpu_custom_call" | custom-call | tf_op jit(solution)/shard_map/pallas_call | solution.py:521
  37.0 1.9 %copy.6 = f32[32,32,32]{2,1,0:T(8,128)} copy(f32[32,32,32]{2,1,0:T(8,128)} %shard_map.46) | data formatting | bytes 262144
where the time goes:
time: 39 us; the launch traced here: 38.9 us
  Pallas kernels  37 us (95%)
  local copies, waits for them, and re-layouts  1.87 us (5%)
    pallas_call x1, Pallas kernels, local(): pl.pallas_call(kernel, out_shape=jax.ShapeDtypeStruct(estimate.shape, F32...  37 us
    unnamed x1, local copies, waits for them, and re-layouts  1.87 us

commit v1 on v0

--- a/solution.py
+++ b/solution.py
@@ -58,13 +58,12 @@
         main = jnp.where(near, band(backward, LANES, -RAD), 0.0)
         low = jnp.where((lane16 < RAD) & (q > 0), band(backward, 16, 0), 0.0)
         high = jnp.where((lane16 < RAD) & (q < 3), band(backward, 16, 96), 0.0)
-        high = pltpu.roll(high, RAD, 1)
         for g in range(GROUPS):
             wb[g, r * 128 : r * 128 + 128, 0:128] = (
                 pltpu.roll(main, 32 * g, 1) if g else main
             ).astype(BF16)
             wb[g, r * 128 : r * 128 + 128, 128:256] = jnp.zeros((128, LANES), BF16)
-            lo, hi = (pltpu.roll(m, 32 * g, 1) if g else m for m in (low, high))
+            lo, hi = pltpu.roll(low, RAD * g, 1) if g else low, pltpu.roll(high, 64 + RAD * g, 1)
             wb[g, r * 128 : r * 128 + 16, 128:256] = lo.astype(BF16)
             wb[g, r * 128 + 112 : r * 128 + 128, 128:256] = hi.astype(BF16)
 
@@ -365,9 +364,8 @@
             )
         return carry
 
-    def backward(half):
+    def backward_x(half):
         rows, within = slice(half * 128, half * 128 + 128), slice(half * 128, half * 128 + 384)
-        rim_sum = None
         for pair in range(2):
             for r in range(RANK):
                 at = r * GROUPS + 2 * pair
@@ -375,13 +373,23 @@
                 done = dot(txb[r, rows, within], both).astype(BF16)
                 for k in range(2):
                     back_x[2 * pair + k, rows, r * 128 : (r + 1) * 128] = done[:, k * 128 : k * 128 + 128]
-            for g in (2 * pair, 2 * pair + 1):
-                done = dot(back_x[g, rows, :], wb[g])
-                for c in range(4):
-                    at = (g + c) % 4
-                    sums[half, c, :, at * 32 : at * 32 + 32] = done[:, at * 32 : at * 32 + 32]
-                rim_sum = done[:, LANES:] if rim_sum is None else rim_sum + done[:, LANES:]
-        return rim_sum
+
+    def backward_rims(half):
+        rows = slice(half * 128, half * 128 + 128)
+        both = dot(back_x[0, rows, :], wb[0, :, LANES:])
+        for g in range(1, GROUPS):
+            both = both + dot(back_x[g, rows, :], wb[g, :, LANES:])
+        is_low = iota((64, LANES), 1) < 64
+        rims[half, 0] = jnp.where(is_low, both[0:64], pltpu.roll(both[64:128], 64, 1))
+        rims[half, 1] = jnp.where(is_low, pltpu.roll(both[0:64], 64, 1), both[64:128])
+
+    def backward_z(half):
+        rows = slice(half * 128, half * 128 + 128)
+        for g in range(GROUPS):
+            done = dot(back_x[g, rows, :], wb[g, :, :LANES])
+            for c in range(4):
+                at = (g + c) % 4
+                sums[half, c, :, at * 32 : at * 32 + 32] = done[:, at * 32 : at * 32 + 32]
 
     far = (1 - chip) * 2 + core
 
@@ -398,38 +406,38 @@
         sum_copy(sums.at[h, chip * 2 + 1 - core], got_core.at[h, 1], 2 + h, partner) for h in range(2)
     ]
     over = [sum_copy(sums.at[h, far], got_chip.at[h], 4 + h, at_vert(q * 4 + far)) for h in range(2)]
-    rim_swap = sum_copy(rims.at[1 - core], got_rim, 6, partner)
+    rim_swap = [sum_copy(rims.at[h, 1 - core], got_rim.at[h], 6 + h, partner) for h in range(2)]
     edge_home = jnp.where(core == 0, vert - slot - 1, vert - slot + 4)
     edge_there = jnp.where(core == 0, q, 3 - q) > 0
 
-    def edge_copy(which):
+    def edge_copy(h, which):
         return pltpu.make_async_remote_copy(
-            src_ref=rims.at[core], dst_ref=got_edge.at[which], send_sem=sum_send.at[7],
-            recv_sem=sum_recv.at[7 + which], device_id=at_vert(edge_home), device_id_type=MESH,
+            src_ref=rims.at[h, core], dst_ref=got_edge.at[which, h], send_sem=sum_send.at[8 + h],
+            recv_sem=sum_recv.at[8 + 2 * h + which], device_id=at_vert(edge_home), device_id_type=MESH,
         )
 
+    def backward(h):
+        backward_x(h)
+        backward_rims(h)
+        rim_swap[h].start()
+        backward_z(h)
+        far_swap[h].start()
+        near_swap[h].start()
+
     def pass_over(h):
+        rim_swap[h].wait_recv()
+        rims[h, core] = rims[h, core] + got_rim[h]
+        pl.when(edge_there)(lambda: edge_copy(h, chip).start())
         far_swap[h].wait_recv()
         sums[h, far] = sums[h, far] + got_core[h, 0]
         over[h].start()
 
     lax.fori_loop(0, 12, along_y, 0, unroll=4)
-    top = backward(0)
-    far_swap[0].start()
-    near_swap[0].start()
+    backward(0)
     lax.fori_loop(12, 16, along_y, 0, unroll=4)
     pass_over(0)
-    bottom = backward(1)
-    far_swap[1].start()
-    is_low = iota((128, LANES), 1) % 32 < RAD
-    rims[0] = jnp.where(is_low, top, pltpu.roll(bottom, RAD, 1))
-    rims[1] = jnp.where(is_low, pltpu.roll(top, LANES - RAD, 1), bottom)
-    rim_swap.start()
-    near_swap[1].start()
+    backward(1)
     pass_over(1)
-    rim_swap.wait_recv()
-    rims[core] = rims[core] + got_rim[...]
-    pl.when(edge_there)(lambda: edge_copy(chip).start())
 
     mine = []
     for h in range(2):
@@ -441,19 +449,23 @@
 
     @pl.when(is_edge)
     def _():
-        edge_copy(0).wait_recv()
-        edge_copy(1).wait_recv()
-
-    edge = got_edge[0] + got_edge[1]
+        for h in range(2):
+            edge_copy(h, 0).wait_recv()
+            edge_copy(h, 1).wait_recv()
+
     start = jnp.where(last, RAD, 0)
-    lane = iota((128, LANES), 1)
+    lane = iota((64, LANES), 1)
     keep = is_edge & (lane >= start) & (lane < start + RAD)
-    for g in range(GROUPS):
-        for h in range(2):
-            rim = pltpu.roll(edge, (start + 2 * LANES - RAD * h - 32 * g) % LANES, 1)
-            own = pltpu.roll(mine[h], (8 - g - slot) % 4 * 32, 1) + jnp.where(keep, rim, 0.0)
-            at = (slice(16 * h, 16 * h + 16), slice(g * 8, g * 8 + 8))
-            refined[at] = est[at] * (own[:, 0:BLOCK].reshape(16, 8, BLOCK) * (1.0 / (RANK * VIEWS)))
+    for h in range(2):
+        edge = got_edge[0, h] + got_edge[1, h]
+        for g in range(GROUPS):
+            own = pltpu.roll(mine[h], (8 - g - slot) % 4 * 32, 1)
+            for k in range(2):
+                rim = pltpu.roll(edge, (start + LANES - 64 * k - RAD * g) % LANES, 1)
+                part = own[64 * k : 64 * k + 64] + jnp.where(keep, rim, 0.0)
+                part = part[:, 0:BLOCK].reshape(8, 8, BLOCK) * (1.0 / (RANK * VIEWS))
+                at = (slice(16 * h + 8 * k, 16 * h + 8 * k + 8), slice(g * 8, g * 8 + 8))
+                refined[at] = est[at] * part
 
     for k in range(1, VIEWS):
         part_copy(slot, k - 1, partner, 0).wait_send()
@@ -473,9 +485,13 @@
                 for tp in range(2):
                     core_copy(jy, jx, tp, core).wait_send()
 
-    for copy in far_swap + near_swap + over + [rim_swap]:
+    for copy in far_swap + near_swap + over + rim_swap:
         copy.wait_send()
-    pl.when(edge_there)(lambda: edge_copy(0).wait_send())
+
+    @pl.when(edge_there)
+    def _():
+        for h in range(2):
+            edge_copy(h, 0).wait_send()
 
 
 def local(estimate, view_tiles, slot_view, psf_taps):
@@ -496,11 +512,11 @@
         pltpu.VMEM((12, 512, LANES), BF16),
         pltpu.VMEM((GROUPS, 256, RANK * LANES), BF16),
         pltpu.VMEM((2, 4, 128, LANES), F32),
+        pltpu.VMEM((2, 2, 64, LANES), F32),
+        pltpu.VMEM((2, 2, 128, LANES), F32),
+        pltpu.VMEM((2, 64, LANES), F32),
         pltpu.VMEM((2, 128, LANES), F32),
-        pltpu.VMEM((2, 2, 128, LANES), F32),
-        pltpu.VMEM((128, LANES), F32),
-        pltpu.VMEM((2, 128, LANES), F32),
-        pltpu.VMEM((2, 128, LANES), F32),
+        pltpu.VMEM((2, 2, 64, LANES), F32),
         pltpu.VMEM((2, 24, LANES), F32),
         pltpu.VMEM((RANK, 256, 512), BF16),
         pltpu.VMEM((RANK, 128, 256), BF16),
@@ -515,19 +531,19 @@
         pltpu.SemaphoreType.DMA((18,)),
         pltpu.SemaphoreType.DMA((18,)),
         pltpu.SemaphoreType.DMA((18,)),
-        pltpu.SemaphoreType.DMA((8,)),
-        pltpu.SemaphoreType.DMA((9,)),
+        pltpu.SemaphoreType.DMA((10,)),
+        pltpu.SemaphoreType.DMA((12,)),
     ]
     return pl.pallas_call(
         kernel,
-        out_shape=jax.ShapeDtypeStruct(estimate.shape, F32),
+        out_shape=pltpu.VMEM(estimate.shape, F32),
         in_specs=[hbm] * 4,
         out_specs=vmem,
         scratch_shapes=scratch,
         compiler_params=pltpu.CompilerParams(
-            collective_id=0, has_side_effects=True, vmem_limit_bytes=64 * 1024 * 1024
+            collective_id=0, has_side_effects=True, vmem_limit_bytes=56 * 1024 * 1024
         ),
-    )(estimate, tile, psf, slot_view)
+    )(*(pltpu.with_memory_space_constraint(a, pltpu.HBM) for a in (estimate, tile, psf, slot_view)))
 
 
 def solution(mesh):

time: 39 us -> 35.9 us (0.921)
  Pallas kernels: 37 us -> 35 us
  local copies, waits for them, and re-layouts: 1.87 us -> 0.8 us
    pallas_call x1, Pallas kernels: 37 us -> 35 us  [local(): pl.pallas_call(kernel, out_shape=pltpu.VMEM(estimate.shape, F32), in_spec...]
    unnamed x1, local copies, waits for them, and re-layouts: 1.87 us -> 0.8 us
where the time goes in v1:
time: 35.9 us; the launch traced here: 35.8 us
  Pallas kernels  35 us (97%)
  local copies, waits for them, and re-layouts  0.8 us (2%)
    pallas_call x1, Pallas kernels, local(): pl.pallas_call(kernel, out_shape=pltpu.VMEM(estimate.shape, F32), in_spec...  35 us
    unnamed x1, local copies, waits for them, and re-layouts  0.8 us

profile of v1, /device:TPU:47, one launch (start us, length us, event | category | flops | bytes accessed | tf_op | source)
XLA Modules:
  0.0 35.8 jit_solution(17227759291673283302)
XLA Ops:
  0.0 35.0 %shard_map.46 = f32[32,32,32]{2,1,0:T(8,128)S(1)} custom-call(f32[32,32,32]{2,1,0:T(8,128)} %est_hbm.1, bf16[64,64,128]{2,1,0:T(8,128)(2,1)} %bitcast.2, f32[3,3,4,33]{3,2,1,0:T(4,128)} %bitcast.3, s32[1,1,4]{2,1,0:T(1,128)} %slot_view_hbm.1), custom_call_target="tpu_custom_call" | custom-call | tf_op jit(solution)/shard_map/pallas_call | solution.py:537
  35.0 0.8 %copy.6 = f32[32,32,32]{2,1,0:T(8,128)} copy(f32[32,32,32]{2,1,0:T(8,128)S(1)} %shard_map.46) | data formatting | bytes 262144
